TPU v7x, 1024 devices: a whole 8x8x8 slice. The times are simulated.
1024 devices in a mesh: dp: 32 (over z, y_hi, core), expert: 32 (over x, y_lo).
Axes of the slice: x: 8, y: 8 (y_hi: 2, y_lo: 4; y = y_hi * 4 + y_lo), z: 8, core: 2. Of those that a mesh axis runs over, the one named last changes fastest.
Arguments:
- tokens: bfloat16 [4096, 3584], P(('dp', 'expert')), may hold values from -6 to 6
- routes: int32 [4096, 2], P(('dp', 'expert')), may hold values from 0 to 3, all different within a row; in each aligned block of 4 rows (0 to 3, 4 to 7, ...) at most 4 rows name the same one
- route_gates: float32 [4096, 2], P(('dp', 'expert')), may hold values from 0.1 to 0.6
- out_grad: bfloat16 [4096, 3584], P(('dp', 'expert')), may hold values from -6 to 6
- w_gate: bfloat16 [3584, 4096], P(None, 'expert'), may hold values from -0.09375 to 0.09375
- w_up: bfloat16 [3584, 4096], P(None, 'expert'), may hold values from -0.09375 to 0.09375
- w_down: bfloat16 [4096, 3584], P('expert'), may hold values from -0.1875 to 0.1875
Outputs:
- moe_out: bfloat16 [4096, 3584], P(('dp', 'expert'))
- token_grad: bfloat16 [4096, 3584], P(('dp', 'expert'))
- grad_gate: bfloat16 [3584, 4096], P('dp', 'expert')
- grad_up: bfloat16 [3584, 4096], P('dp', 'expert')
- grad_down: bfloat16 [4096, 3584], P('expert', 'dp')
Inputs may be any that keep to these rules, and one draw needn't show every extreme that they name: `routes`: each row names 2 different experts; among the rows of one device no expert is named by more than 4 rows, a bound that some block reaches.
All inputs are finite; a program needn't handle non-finite values.
Results may differ from a plain program's by a relative error of at most 0.02.
Values may be sent and summed in bfloat16 or wider, within the bound.
A program may use at most 32 MiB of HBM per device.

v0:
```python
import jax
import jax.numpy as jnp
from jax import lax
from jax.sharding import PartitionSpec as P


def local(tokens, routes, route_gates, out_grad, w_gate, w_up, w_down):
    n_devices = lax.axis_size("expert")
    slices = min(8, n_devices // 2)
    n_experts = n_devices // slices
    tok_rows = tokens.shape[0]
    top_count = routes.shape[1]
    capacity = tok_rows * top_count * 2 // n_experts
    width = tokens.shape[1]
    expert_ids = jnp.arange(n_experts, dtype=jnp.int32)
    hit = routes[:, :, None] == expert_ids[None, None, :]
    chosen = jnp.any(hit, axis=1).astype(jnp.int32)
    gate_table = jnp.sum(jnp.where(hit, route_gates[:, :, None], jnp.float32(0.0)), axis=1)
    slot_index = jnp.cumsum(chosen, axis=0) - 1
    placed = (chosen[:, :, None] == 1) & (
        slot_index[:, :, None] == jnp.arange(capacity, dtype=jnp.int32)[None, None, :]
    )
    place_f = placed.astype(jnp.float32)
    gated_place = place_f * gate_table[:, :, None]
    send_rows = jnp.einsum(
        "tec,td->ecd", placed.astype(jnp.bfloat16), tokens, preferred_element_type=jnp.float32
    ).astype(jnp.bfloat16)
    send_grad = jnp.einsum("tec,td->ecd", gated_place, out_grad.astype(jnp.float32)).astype(
        jnp.bfloat16
    )
    send_rows = jnp.repeat(send_rows, slices, axis=0)
    send_grad = jnp.repeat(send_grad, slices, axis=0)
    recv_rows, recv_grad = (
        lax.all_to_all(send_rows, "expert", split_axis=0, concat_axis=0, tiled=True),
        lax.all_to_all(send_grad, "expert", split_axis=0, concat_axis=0, tiled=True),
    )
    rows = recv_rows.reshape(-1, width)
    slot_grad = recv_grad.reshape(-1, width)
    a_val = jnp.dot(rows, w_gate, preferred_element_type=jnp.float32)
    b_val = jnp.dot(rows, w_up, preferred_element_type=jnp.float32)
    sig = jax.nn.sigmoid(a_val)
    act = a_val * sig
    hidden = (act * b_val).astype(jnp.bfloat16)
    part_down = (
        jnp.dot(hidden.T, slot_grad, preferred_element_type=jnp.float32)
        .astype(jnp.bfloat16)
        .astype(jnp.float32)
    )
    out = jnp.dot(hidden, w_down, preferred_element_type=jnp.float32).astype(jnp.bfloat16)
    d_hidden = jnp.dot(slot_grad, w_down.T, preferred_element_type=jnp.float32)
    d_up = (d_hidden * act).astype(jnp.bfloat16)
    d_gate = (d_hidden * b_val * sig * (1.0 + a_val * (1.0 - sig))).astype(jnp.bfloat16)
    part_gate = (
        jnp.dot(rows.T, d_gate, preferred_element_type=jnp.float32)
        .astype(jnp.bfloat16)
        .astype(jnp.float32)
    )
    part_up = (
        jnp.dot(rows.T, d_up, preferred_element_type=jnp.float32)
        .astype(jnp.bfloat16)
        .astype(jnp.float32)
    )
    d_rows = (
        jnp.dot(d_gate, w_gate.T, preferred_element_type=jnp.float32)
        + jnp.dot(d_up, w_up.T, preferred_element_type=jnp.float32)
    ).astype(jnp.bfloat16)
    back_out, back_dx = (
        lax.all_to_all(
            out.reshape(n_devices, capacity, width),
            "expert",
            split_axis=0,
            concat_axis=0,
            tiled=True,
        ),
        lax.all_to_all(
            d_rows.reshape(n_devices, capacity, width),
            "expert",
            split_axis=0,
            concat_axis=0,
            tiled=True,
        ),
    )
    out_total = jnp.sum(
        back_out.astype(jnp.float32).reshape(n_experts, slices, capacity, width), axis=1
    )
    dx_total = jnp.sum(
        back_dx.astype(jnp.float32).reshape(n_experts, slices, capacity, width), axis=1
    )
    moe_out = jnp.einsum("tec,ecd->td", gated_place, out_total).astype(jnp.bfloat16)
    token_grad = jnp.einsum("tec,ecd->td", place_f, dx_total).astype(jnp.bfloat16)
    summed_gate, summed_up, summed_down = (
        lax.psum_scatter(
            part_gate.astype(jnp.bfloat16), "dp", scatter_dimension=0, tiled=True
        ).astype(jnp.float32),
        lax.psum_scatter(
            part_up.astype(jnp.bfloat16), "dp", scatter_dimension=0, tiled=True
        ).astype(jnp.float32),
        lax.psum_scatter(
            part_down.astype(jnp.bfloat16), "dp", scatter_dimension=1, tiled=True
        ).astype(jnp.float32),
    )
    return (
        moe_out,
        token_grad,
        summed_gate.astype(jnp.bfloat16),
        summed_up.astype(jnp.bfloat16),
        summed_down.astype(jnp.bfloat16),
    )


def solution(mesh):
    return jax.shard_map(
        local,
        mesh=mesh,
        in_specs=(
            P(("dp", "expert"), None),
            P(("dp", "expert"), None),
            P(("dp", "expert"), None),
            P(("dp", "expert"), None),
            P(None, "expert"),
            P(None, "expert"),
            P("expert", None),
        ),
        out_specs=(
            P(("dp", "expert"), None),
            P(("dp", "expert"), None),
            P("dp", "expert"),
            P("dp", "expert"),
            P("expert", "dp"),
        ),
        check_vma=False,
    )
```

profile of v0, /device:TPU:1, one launch (start us, length us, event | category | flops | bytes accessed | tf_op | source)
XLA Modules:
  0.0 503.5 jit_solution(15015790846078752082)
XLA Ops:
  7.2 0.0 copy-start
  7.2 0.0 copy-start.5
  7.2 0.8 fusion.9
  8.0 0.8 select_reduce_fusion
  8.9 0.1 copy.22
  9.0 0.9 convolution_convert_fusion.5
  9.9 1.2 broadcast_in_dim.27
  11.1 11.1 %all-to-all-start = ((bf16[32,4,3584]{2,1,0:T(4,128)(2,1)}), bf16[32,4,3584]{2,1,0:T(4,128)(2,1)S(1)}, u32[]{:S(2)}, u32[]{:S(2)}) async-start(bf16[32,4,3584]{2,1,0:T(4,128)(2,1)} %bitcast.1), calls=%async_computation | async-start | bytes 1835008 | tf_op jit(solution)/shard_map/all_to_all | solution.py:34
  22.2 0.1 copy.24
  22.3 0.0 copy-done.5
  22.3 0.2 convolution_convert_fusion.4
  22.5 17.7 %all-to-all-done = bf16[32,4,3584]{2,1,0:T(4,128)(2,1)S(1)} async-done(((bf16[32,4,3584]{2,1,0:T(4,128)(2,1)}), bf16[32,4,3584]{2,1,0:T(4,128)(2,1)S(1)}, u32[]{:S(2)}, u32[]{:S(2)}) %all-to-all-start) | async-done | bytes 917536 | tf_op jit(solution)/shard_map/all_to_all | solution.py:34
  40.1 0.0 copy-start.3
  40.1 1.3 broadcast_in_dim.28
  41.4 0.0 copy-start.1
  41.4 12.8 %all-to-all-start.2 = ((bf16[32,4,3584]{2,1,0:T(4,128)(2,1)}), bf16[32,4,3584]{2,1,0:T(4,128)(2,1)}, u32[]{:S(2)}, u32[]{:S(2)}) async-start(bf16[32,4,3584]{2,1,0:T(4,128)(2,1)} %bitcast.43), calls=%async_computation.2 | async-start | bytes 1835008 | tf_op jit(solution)/shard_map/all_to_all | solution.py:35
  54.3 0.0 copy-done.3
  54.3 0.0 reduce-scatter.8.cloned.1.call-start
  54.3 1.7 reshape.58
  56.0 0.0 copy-done.1
  56.0 0.0 copy-start.4
  56.0 0.4 fusion.13
  56.4 0.8 copy-done.4
  57.2 0.4 fusion.12
  57.6 20.7 %all-to-all-done.2 = bf16[32,4,3584]{2,1,0:T(4,128)(2,1)} async-done(((bf16[32,4,3584]{2,1,0:T(4,128)(2,1)}), bf16[32,4,3584]{2,1,0:T(4,128)(2,1)}, u32[]{:S(2)}, u32[]{:S(2)}) %all-to-all-start.2) | async-done | bytes 917536 | tf_op jit(solution)/shard_map/all_to_all | solution.py:35
  78.3 1.7 reshape.63
  80.0 0.0 copy-done
  80.0 0.4 multiply_convert_fusion
  80.4 1.4 convolution_convert_fusion
  81.8 0.0 reduce-scatter.8.cloned.1.call-update
  81.8 0.0 copy-start.2
  81.8 1.7 fusion.14
  83.5 0.0 copy-done.2
  83.5 0.4 fusion
  83.9 1.2 reshape.64
  85.1 6.7 %all-to-all-start.3 = ((bf16[32,4,3584]{2,1,0:T(4,128)(2,1)}), bf16[32,4,3584]{2,1,0:T(4,128)(2,1)}, u32[]{:S(2)}, u32[]{:S(2)}) async-start(bf16[32,4,3584]{2,1,0:T(4,128)(2,1)} %reshape.64), calls=%async_computation.3 | async-start | bytes 1835008 | tf_op jit(solution)/shard_map/all_to_all | solution.py:75
  91.8 0.0 reduce-scatter.4.cloned.1.call-start
  91.9 1.4 convolution_convert_fusion.2
  93.3 0.0 reduce-scatter.4.cloned.1.call-update
  93.3 0.4 convolution_convert_fusion.3
  93.7 1.1 reshape.59
  94.8 21.2 %all-to-all-done.3 = bf16[32,4,3584]{2,1,0:T(4,128)(2,1)} async-done(((bf16[32,4,3584]{2,1,0:T(4,128)(2,1)}), bf16[32,4,3584]{2,1,0:T(4,128)(2,1)}, u32[]{:S(2)}, u32[]{:S(2)}) %all-to-all-start.3) | async-done | bytes 917536 | tf_op jit(solution)/shard_map/all_to_all | solution.py:75
  116.0 6.5 %all-to-all-start.1 = ((bf16[32,4,3584]{2,1,0:T(4,128)(2,1)}), bf16[32,4,3584]{2,1,0:T(4,128)(2,1)S(1)}, u32[]{:S(2)}, u32[]{:S(2)}) async-start(bf16[32,4,3584]{2,1,0:T(4,128)(2,1)} %reshape.59), calls=%async_computation.1 | async-start | bytes 1835008 | tf_op jit(solution)/shard_map/all_to_all | solution.py:68
  122.5 0.0 reduce-scatter.6.cloned.1.call-start
  122.5 1.4 convolution_convert_fusion.1
  123.9 0.0 reduce-scatter.6.cloned.1.call-update
  123.9 1.6 convert_reduce_fusion
  125.6 0.9 fusion.2
  126.4 20.3 %all-to-all-done.1 = bf16[32,4,3584]{2,1,0:T(4,128)(2,1)S(1)} async-done(((bf16[32,4,3584]{2,1,0:T(4,128)(2,1)}), bf16[32,4,3584]{2,1,0:T(4,128)(2,1)S(1)}, u32[]{:S(2)}, u32[]{:S(2)}) %all-to-all-start.1) | async-done | bytes 917536 | tf_op jit(solution)/shard_map/all_to_all | solution.py:68
  146.7 0.4 convert_reduce_fusion.1
  147.1 0.8 fusion.1
  148.0 73.9 %reduce-scatter.8.cloned.1.call-done = bf16[128,112]{0,1:T(8,128)(2,1)} async-done(((bf16[128,3584]{0,1:T(8,128)(2,1)}), bf16[128,112]{0,1:T(8,128)(2,1)}) %reduce-scatter.8.cloned.1.call-update) | async-done | bytes 28688 | tf_op jit(solution)/shard_map/reduce_scatter | solution.py:98
  221.9 138.0 %reduce-scatter.4.cloned.1.call-done = bf16[112,128]{1,0:T(8,128)(2,1)} async-done(((bf16[3584,128]{1,0:T(8,128)(2,1)}), bf16[112,128]{1,0:T(8,128)(2,1)}) %reduce-scatter.4.cloned.1.call-update) | async-done | bytes 28688 | tf_op jit(solution)/shard_map/reduce_scatter | solution.py:92
  359.9 137.1 %reduce-scatter.6.cloned.1.call-done = bf16[112,128]{1,0:T(8,128)(2,1)} async-done(((bf16[3584,128]{1,0:T(8,128)(2,1)}), bf16[112,128]{1,0:T(8,128)(2,1)}) %reduce-scatter.6.cloned.1.call-update) | async-done | bytes 28688 | tf_op jit(solution)/shard_map/reduce_scatter | solution.py:95
  (4 shorter events, 0.1 us)
Async XLA Ops:
  7.2 72.8 %copy-start = (bf16[128,3584]{1,0:T(8,128)(2,1)S(1)}, bf16[128,3584]{1,0:T(8,128)(2,1)}, u32[]{:S(2)}) copy-start(bf16[128,3584]{1,0:T(8,128)(2,1)} %param.13) | copy-start | bytes 2752516
  7.2 15.1 %copy-start.5 = (bf16[4,3584]{1,0:T(4,128)(2,1)S(1)}, bf16[4,3584]{1,0:T(4,128)(2,1)}, u32[]{:S(2)}) copy-start(bf16[4,3584]{1,0:T(4,128)(2,1)} %param.10) | copy-start | bytes 86020
  11.1 29.1 %all-to-all-start = ((bf16[32,4,3584]{2,1,0:T(4,128)(2,1)}), bf16[32,4,3584]{2,1,0:T(4,128)(2,1)S(1)}, u32[]{:S(2)}, u32[]{:S(2)}) async-start(bf16[32,4,3584]{2,1,0:T(4,128)(2,1)} %bitcast.1), calls=%async_computation | async-start | bytes 1835008 | tf_op jit(solution)/shard_map/all_to_all | solution.py:34
  40.1 14.1 %copy-start.3 = (bf16[32,4,3584]{2,1,0:T(4,128)(2,1)}, bf16[32,4,3584]{2,1,0:T(4,128)(2,1)S(1)}, u32[]{:S(2)}) copy-start(bf16[32,4,3584]{2,1,0:T(4,128)(2,1)S(1)} %all-to-all-done) | copy-start | bytes 2752516
  41.4 14.6 %copy-start.1 = (bf16[3584,128]{1,0:T(8,128)(2,1)S(1)}, bf16[3584,128]{1,0:T(8,128)(2,1)}, u32[]{:S(2)}) copy-start(bf16[3584,128]{1,0:T(8,128)(2,1)} %param.12) | copy-start | bytes 2752516
  41.4 36.9 %all-to-all-start.2 = ((bf16[32,4,3584]{2,1,0:T(4,128)(2,1)}), bf16[32,4,3584]{2,1,0:T(4,128)(2,1)}, u32[]{:S(2)}, u32[]{:S(2)}) async-start(bf16[32,4,3584]{2,1,0:T(4,128)(2,1)} %bitcast.43), calls=%async_computation.2 | async-start | bytes 1835008 | tf_op jit(solution)/shard_map/all_to_all | solution.py:35
  54.3 167.6 %reduce-scatter.8.cloned.1.call-start = ((), (), s32[]{:S(2)}) async-start(), calls=%async_computation.9 | async-start | bytes 946176 | tf_op jit(solution)/shard_map/reduce_scatter | solution.py:98
  56.0 1.2 copy-start.4
  81.8 1.7 copy-start.2
  85.1 30.9 %all-to-all-start.3 = ((bf16[32,4,3584]{2,1,0:T(4,128)(2,1)}), bf16[32,4,3584]{2,1,0:T(4,128)(2,1)}, u32[]{:S(2)}, u32[]{:S(2)}) async-start(bf16[32,4,3584]{2,1,0:T(4,128)(2,1)} %reshape.64), calls=%async_computation.3 | async-start | bytes 1835008 | tf_op jit(solution)/shard_map/all_to_all | solution.py:75
  91.8 268.1 %reduce-scatter.4.cloned.1.call-start = ((), (), s32[]{:S(2)}) async-start(), calls=%async_computation.7 | async-start | bytes 946176 | tf_op jit(solution)/shard_map/reduce_scatter | solution.py:92
  116.0 30.7 %all-to-all-start.1 = ((bf16[32,4,3584]{2,1,0:T(4,128)(2,1)}), bf16[32,4,3584]{2,1,0:T(4,128)(2,1)S(1)}, u32[]{:S(2)}, u32[]{:S(2)}) async-start(bf16[32,4,3584]{2,1,0:T(4,128)(2,1)} %reshape.59), calls=%async_computation.1 | async-start | bytes 1835008 | tf_op jit(solution)/shard_map/all_to_all | solution.py:68
  122.5 374.5 %reduce-scatter.6.cloned.1.call-start = ((), (), s32[]{:S(2)}) async-start(), calls=%async_computation.8 | async-start | bytes 946176 | tf_op jit(solution)/shard_map/reduce_scatter | solution.py:95
Sparse Core Ops, SparseCore 0:
  81.9 139.8 reduce-scatter.7
  229.2 130.6 reduce-scatter.3
  366.2 130.6 reduce-scatter.5
where the time goes:
time: 509 us; the launch traced here: 503 us
  waiting for transfers between devices  429 us (84%)
  starting transfers between devices  37.2 us (7%)
  between operations  13.9 us (3%)
  matrix products  10.6 us (2%)
  local copies, waits for them, and re-layouts  9.1 us (2%)
    reduce_scatter x1, waiting for transfers between devices, local(): lax.psum_scatter(part_gate.astype(jnp.bfloat16), 'dp', scatter_dimension=...  138 us
    reduce_scatter x1, waiting for transfers between devices, local(): lax.psum_scatter(part_up.astype(jnp.bfloat16), 'dp', scatter_dimension=0,...  137 us
    reduce_scatter x1, waiting for transfers between devices, local(): lax.psum_scatter(part_down.astype(jnp.bfloat16), 'dp', scatter_dimension=...  73.9 us
    all_to_all x1, waiting for transfers between devices, local(): lax.all_to_all(d_rows.reshape(n_devices, capacity, width), 'expert', spli...  21.2 us
    all_to_all x1, waiting for transfers between devices, local(): lax.all_to_all(send_grad, 'expert', split_axis=0, concat_axis=0, tiled=True)  20.7 us
    all_to_all x1, waiting for transfers between devices, local(): lax.all_to_all(out.reshape(n_devices, capacity, width), 'expert', split_a...  20.3 us
    all_to_all x1, waiting for transfers between devices, local(): lax.all_to_all(send_rows, 'expert', split_axis=0, concat_axis=0, tiled=True)  17.7 us
    all_to_all x1, starting transfers between devices, local(): lax.all_to_all(send_grad, 'expert', split_axis=0, concat_axis=0, tiled=True)  12.8 us
  transfers between devices with their start and end apart: 7, of which 7 were waited for; matrix products, arithmetic and copies ran while one was open for 3% of the time, Pallas kernels for 0%

commit v1 on v0

v1 whole, which is shorter than its diff:
```python
import jax
import jax.numpy as jnp
from jax import lax
from jax.experimental import pallas as pl
from jax.experimental.pallas import tpu as pltpu
from jax.sharding import PartitionSpec as P

NX, NY, NZ, NH, NC = 8, 4, 8, 2, 2
EXPERTS = 4
SEG = 4
NB = 4
BF, F32 = jnp.bfloat16, jnp.float32
NN, NT, TN = (((1,), (0,)), ((), ())), (((1,), (1,)), ((), ())), (((0,), (0,)), ((), ()))


def mm(a, b, dims=NN, precision=None):
    return lax.dot_general(a, b, dims, precision=precision, preferred_element_type=F32)


def iota(shape, dim):
    return lax.broadcasted_iota(jnp.int32, shape, dim)


def split(n, tile):
    return -(-(n // tile) // 2) * tile


def build(tok, d, ff):
    lt, le = tok.bit_length() - 1, EXPERTS.bit_length() - 1
    ly = NY.bit_length() - 1
    seg_w = d // SEG
    chunk = SEG * tok
    brow = NY * tok
    rows = NX * brow
    hx, hz = NX // 2, NZ // 2
    bw, zb = d // NB, NZ // NB
    dr = d // (NZ * NH * NC)
    gr = 3 * dr
    ds = split(d, 128)
    gs = split(gr, 16)
    kb = 512
    n_copies = 9 * NY + 5 * 2 * hx + NB + 2 * 2 * hz + 4

    def kernel(
        tok_ref, routes_ref, gates_ref, og_ref, wg_hbm, wu_hbm, wd_hbm,
        out_ref, dx_ref, gg_ref, gu_ref, gd_ref,
        wgu, wd, xc, dc, gc, xy, dy, gy, xg, dg, gx, sdo,
        o_part, d_part, o_in, d_in, oc, xo, oy, xdy,
        gp, gcin, zsum, zin, hout, hin,
        wsem, ssem, rsem,
    ):
        dp, ei = lax.axis_index("dp"), lax.axis_index("expert")
        x, y = ei // NY, ei % NY
        z, h, c = dp // (NH * NC), (dp // NC) % NH, dp % NC

        def at_x(v):
            return (dp, v * NY + y)

        def at_y(v):
            return (dp, x * NY + v)

        def at_z(v):
            return ((v * NH + h) * NC + c, ei)

        right, left = at_x((x + 1) % NX), at_x((x + NX - 1) % NX)
        up, down = at_z((z + 1) % NZ), at_z((z + NZ - 1) % NZ)
        other_h = ((z * NH + 1 - h) * NC + c, ei)
        other_c = ((z * NH + h) * NC + 1 - c, ei)
        partners = [at_y((y + k) % NY) for k in range(1, NY)]
        partners += [right, left, up, down, other_h, other_c]

        barrier = pltpu.get_barrier_semaphore()
        for p in partners:
            pl.semaphore_signal(barrier, inc=1, device_id=p, device_id_type=pl.DeviceIdType.MESH)

        loads = [
            pltpu.make_async_copy(wg_hbm, wgu.at[:, 0:ff], wsem.at[0]),
            pltpu.make_async_copy(wu_hbm, wgu.at[:, ff : 2 * ff], wsem.at[1]),
            pltpu.make_async_copy(wd_hbm, wd, wsem.at[2]),
        ]
        for load in loads:
            load.start()

        sent = []
        ids = {}

        def copy(key, src, dst, dev):
            n = ids.setdefault(key, len(ids))
            return pltpu.make_async_remote_copy(
                src_ref=src, dst_ref=dst, send_sem=ssem.at[n], recv_sem=rsem.at[n],
                device_id=dev, device_id_type=pl.DeviceIdType.MESH,
            )

        def send(key, src, dst, dev):
            op = copy(key, src, dst, dev)
            op.start()
            sent.append(op)

        def arrive(key, dst, dev):
            copy(key, dst, dst, dev).wait_recv()

        def pack(ref):
            total = None
            for s in range(SEG):
                place = (iota((chunk, tok), 0) == iota((chunk, tok), 1) + s * tok).astype(BF)
                term = mm(place, ref[:, s * seg_w : (s + 1) * seg_w])
                total = term if total is None else total + term
            return total.astype(BF)

        xc[...] = pack(tok_ref)
        lane, row = iota((tok, 128), 1), iota((tok, 128), 0)
        table = jnp.zeros((tok, 128), F32)
        for k in range(routes_ref.shape[1]):
            mine = ((lane >> le) == row) & ((lane & (EXPERTS - 1)) == routes_ref[:, k : k + 1])
            table = table + jnp.where(mine, gates_ref[:, k : k + 1], 0.0)
        line = jnp.sum(table, axis=0, keepdims=True)
        gc[...] = jnp.where(iota((8, 128), 0) == y, line, 0.0)

        pl.semaphore_wait(barrier, len(partners))

        for k in range(1, NY):
            send(("yx", k), xc, xy.at[y], at_y((y + k) % NY))
        for k in range(1, NY):
            send(("yg", k), gc, gy.at[y], at_y((y + k) % NY))
        dc[...] = pack(og_ref)
        for k in range(1, NY):
            send(("yd", k), dc, dy.at[y], at_y((y + k) % NY))

        def place_of(s):
            r, q = iota((brow, NY * chunk), 0), iota((brow, NY * chunk), 1)
            return (q == (r >> lt) * chunk + s * tok + (r & (tok - 1))).astype(BF)

        def xrows(v):
            return pl.ds(pl.multiple_of((v % NX) * brow, brow), brow)

        def unpack_to(buf, own, dst):
            buf[pl.ds(y, 1)] = own[...][None]
            all_rows = buf[...].reshape(NY * chunk, seg_w)
            for s in range(SEG):
                dst[xrows(x), s * seg_w : (s + 1) * seg_w] = mm(place_of(s), all_rows).astype(BF)

        def gather_views(name, s):
            buf = {"x": xg, "d": dg}[name]
            r_cols, l_cols = (slice(0, ds), slice(ds, d)) if s == hx else (slice(0, d), slice(0, d))
            return buf, r_cols, l_cols

        def gather_send(name, s):
            buf, rc, lc = gather_views(name, s)
            v = buf.at[xrows(x + NX - s + 1), rc]
            send((name, "r", s), v, v, right)
            v = buf.at[xrows(x + s - 1), lc]
            send((name, "l", s), v, v, left)

        def gather_arrive(name, s):
            buf, rc, lc = gather_views(name, s)
            arrive((name, "r", s), buf.at[xrows(x + NX - s), rc], right)
            arrive((name, "l", s), buf.at[xrows(x + s), lc], left)

        def gate_send(s):
            v = gx.at[(x + NX - s + 1) % NX]
            send(("g", "r", s), v, v, right)
            if s < hx:
                v = gx.at[(x + s - 1) % NX]
                send(("g", "l", s), v, v, left)

        def gate_arrive(s):
            arrive(("g", "r", s), gx.at[(x + NX - s) % NX], right)
            if s < hx:
                arrive(("g", "l", s), gx.at[(x + s) % NX], left)

        for k in range(1, NY):
            arrive(("yx", k), xy.at[(y + NY - k) % NY], at_y((y + k) % NY))
        unpack_to(xy, xc, xg)
        gather_send("x", 1)
        for k in range(1, NY):
            arrive(("yg", k), gy.at[(y + NY - k) % NY], at_y((y + k) % NY))
        gy[pl.ds(y, 1)] = gc[...][None]
        gx[pl.ds(x, 1)] = jnp.sum(gy[...], axis=0, keepdims=True)
        gate_send(1)
        for k in range(1, NY):
            arrive(("yd", k), dy.at[(y + NY - k) % NY], at_y((y + k) % NY))
        unpack_to(dy, dc, dg)
        gather_send("d", 1)
        for s in range(1, hx):
            gather_arrive("x", s)
            gather_send("x", s + 1)
            gate_arrive(s)
            gate_send(s + 1)
            gather_arrive("d", s)
            gather_send("d", s + 1)
        gather_arrive("x", hx)
        gate_arrive(hx)

        expert = ei // (NX * NY // EXPERTS)
        t, q = iota((rows, NX * 8), 0), iota((rows, NX * 8), 1)
        pick = (q == (t >> (lt + ly)) * 8 + ((t >> lt) & (NY - 1))).astype(F32)
        picked = mm(pick, gx[...].reshape(NX * 8, 128), precision=lax.Precision.HIGHEST)
        t, q = iota((rows, 128), 0), iota((rows, 128), 1)
        mine = q == (t & (tok - 1)) * EXPERTS + expert
        gate = jnp.sum(jnp.where(mine, picked, 0.0), axis=1, keepdims=True)

        loads[0].wait()
        loads[1].wait()
        ab = jnp.zeros((rows, 2 * ff), F32)
        for i in range(0, d, kb):
            ab = ab + mm(xg[:, i : i + kb], wgu[i : i + kb, :])
        a, b = ab[:, 0:ff], ab[:, ff : 2 * ff]
        sig = jax.nn.sigmoid(a)
        act = a * sig
        hidden = (act * b).astype(BF)
        loads[2].wait()
        for i in range(0, d, kb):
            o_part[:, i : i + kb] = (mm(hidden, wd[:, i : i + kb]) * gate).astype(BF)

        def scatter_start(name, part, into):
            v = part.at[xrows(x + hx), 0:ds]
            send((name, "r", 1), v, into.at[0, 0, :, 0:ds], right)
            v = part.at[xrows(x + hx), ds:d]
            send((name, "l", 1), v, into.at[1, 0, :, ds:d], left)

        def scatter_step(name, part, into, s):
            for i, (way, dev) in enumerate((("r", right), ("l", left))):
                cols = slice(0, d) if s > 1 else slice(ds, d) if i else slice(0, ds)
                arrive((name, way, s), into.at[i, s - 1, :, cols], dev)
                at = xrows(x + hx - s) if i == 0 else xrows(x + NX - hx + s)
                total = part[at, cols].astype(F32) + into[i, s - 1, :, cols].astype(F32)
                part[at, cols] = total.astype(BF)
                send((name, way, s + 1), part.at[at], into.at[i, s], dev)

        def scatter_end(name, part, into):
            arrive((name, "r", hx), into.at[0, hx - 1], right)
            arrive((name, "l", hx), into.at[1, hx - 1], left)
            total = part[xrows(x), :].astype(F32) + into[0, hx - 1].astype(F32)
            return (total + into[1, hx - 1].astype(F32)).astype(BF)

        scatter_start("o", o_part, o_in)

        gather_arrive("d", hx)
        dh = jnp.zeros((rows, ff), F32)
        for i in range(0, d, kb):
            v = (dg[:, i : i + kb].astype(F32) * gate).astype(BF)
            sdo[:, i : i + kb] = v
            dh = dh + mm(v, wd[:, i : i + kb], NT)
        d_up = (dh * act).astype(BF)
        d_gate = (dh * b * sig * (1.0 + a * (1.0 - sig))).astype(BF)
        dgu = jnp.concatenate([d_gate, d_up], axis=1)

        order = [NB // 2, *(v for k in range(1, NB // 2) for v in (k, NB - k)), 0]

        def core_views(k):
            zs = pl.ds(((z // zb + order[k]) % NB) * zb, zb)
            return zs, gcin.at[zs]

        for k in range(NB):
            block = (z // zb + order[k]) % NB
            cols = pl.ds(pl.multiple_of(block * bw, bw), bw)
            pgu = mm(xg[:, cols], dgu, TN).astype(BF)
            pd = mm(sdo[:, cols], hidden, TN).astype(BF)
            for zz in range(zb):
                for hh in range(NH):
                    for cc in range(NC):
                        at = slice(((zz * NH + hh) * NC + cc) * dr, ((zz * NH + hh) * NC + cc + 1) * dr)
                        gp[cc, block * zb + zz, hh, 0:dr] = pgu[at, 0:ff]
                        gp[cc, block * zb + zz, hh, dr : 2 * dr] = pgu[at, ff : 2 * ff]
                        gp[cc, block * zb + zz, hh, 2 * dr : gr] = pd[at]
            zs, dst = core_views(k)
            send(("c", k), gp.at[1 - c, zs], dst, other_c)

        for i in range(0, d, kb):
            d_part[:, i : i + kb] = mm(dgu, wgu[i : i + kb, :], NT).astype(BF)
        scatter_start("dx", d_part, d_in)

        def both(zd, hh, at):
            return gp[c, zd, hh, at].astype(F32) + gcin[zd, hh, at].astype(F32)

        every, low, high = slice(0, gr), slice(0, gs), slice(gs, gr)

        def z_start(k, hh):
            zd = (z + hz) % NZ
            zsum[zd, hh] = both(zd, hh, every).astype(BF)
            send(("z", k, "u", 1), zsum.at[zd, hh, low], zin.at[k, 0, 0, low], up)
            send(("z", k, "d", 1), zsum.at[zd, hh, high], zin.at[k, 1, 0, high], down)

        def z_step(k, hh, s):
            for i, (way, dev) in enumerate((("u", up), ("d", down))):
                zd = (z + hz - s) % NZ if i == 0 else (z + NZ - hz + s) % NZ
                with_in = every if s > 1 else high if i else low
                arrive(("z", k, way, s), zin.at[k, i, s - 1, with_in], dev)
                total = both(zd, hh, with_in) + zin[k, i, s - 1, with_in].astype(F32)
                zsum[zd, hh, with_in] = total.astype(BF)
                if s == 1:
                    rest = low if i else high
                    zsum[zd, hh, rest] = both(zd, hh, rest).astype(BF)
                send(("z", k, way, s + 1), zsum.at[zd, hh], zin.at[k, i, s], dev)

        def z_end(k, hh):
            arrive(("z", k, "u", hz), zin.at[k, 0, hz - 1], up)
            arrive(("z", k, "d", hz), zin.at[k, 1, hz - 1], down)
            total = both(z, hh, every) + zin[k, 0, hz - 1].astype(F32)
            return total + zin[k, 1, hz - 1].astype(F32)

        zs, dst = core_views(0)
        arrive(("c", 0), dst, other_c)
        z_start(0, 1 - h)
        z_start(1, h)
        for k in range(1, NB):
            zs, dst = core_views(k)
            arrive(("c", k), dst, other_c)

        for s in range(1, max(hx, hz)):
            if s < hz:
                z_step(0, 1 - h, s)
            if s < hx:
                scatter_step("o", o_part, o_in, s)
            if s < hz:
                z_step(1, h, s)
            if s < hx:
                scatter_step("dx", d_part, d_in, s)

        def line_start(name, total, pieces, into):
            spread = None
            for s in range(SEG):
                term = mm(place_of(s), total[:, s * seg_w : (s + 1) * seg_w], TN)
                spread = term if spread is None else spread + term
            pieces[...] = spread.astype(BF).reshape(NY, chunk, seg_w)
            for k in range(1, NY):
                dst_y = (y + k) % NY
                send((name, k), pieces.at[dst_y], into.at[k - 1], at_y(dst_y))

        def line_end(name, pieces, into, result):
            total = pieces[pl.ds(y, 1)].reshape(chunk, seg_w).astype(F32)
            for k in range(1, NY):
                arrive((name, k), into.at[k - 1], at_y((y + k) % NY))
                total = total + into[k - 1].astype(F32)
            total = total.astype(BF)
            for s in range(SEG):
                r, q = iota((chunk, chunk), 0), iota((chunk, chunk), 1)
                back = ((q == r + s * tok) & (r < tok)).astype(BF)
                result[:, s * seg_w : (s + 1) * seg_w] = mm(back, total)[0:tok].astype(BF)

        hout[...] = z_end(0, 1 - h).astype(BF)
        send(("h",), hout, hin, other_h)
        line_start("oy", scatter_end("o", o_part, o_in), oc, oy)
        line_start("xy2", scatter_end("dx", d_part, d_in), xo, xdy)
        total = z_end(1, h)
        line_end("oy", oc, oy, out_ref)
        line_end("xy2", xo, xdy, dx_ref)
        arrive(("h",), hin, other_h)
        total = (total + hin[...].astype(F32)).astype(BF)
        gg_ref[...] = total[0:dr]
        gu_ref[...] = total[dr : 2 * dr]
        eye = (iota((dr, dr), 0) == iota((dr, dr), 1)).astype(BF)
        gd_ref[...] = mm(total[2 * dr : gr], eye, TN).astype(BF)

        for op in sent:
            op.wait_send()
        assert len(ids) <= n_copies

    def vm(shape, dtype=BF):
        return pltpu.VMEM(shape, dtype)

    scratch = [
        vm((d, 2 * ff)), vm((ff, d)),
        vm((chunk, seg_w)), vm((chunk, seg_w)), vm((8, 128), F32),
        vm((NY, chunk, seg_w)), vm((NY, chunk, seg_w)), vm((NY, 8, 128), F32),
        vm((rows, d)), vm((rows, d)), vm((NX, 8, 128), F32), vm((rows, d)),
        vm((rows, d)), vm((rows, d)), vm((2, hx, brow, d)), vm((2, hx, brow, d)),
        vm((NY, chunk, seg_w)), vm((NY, chunk, seg_w)),
        vm((NY - 1, chunk, seg_w)), vm((NY - 1, chunk, seg_w)),
        vm((NC, NZ, NH, gr, ff)), vm((NZ, NH, gr, ff)), vm((NZ, NH, gr, ff)),
        vm((2, 2, hz, gr, ff)), vm((gr, ff)), vm((gr, ff)),
        pltpu.SemaphoreType.DMA((3,)),
        pltpu.SemaphoreType.DMA((n_copies,)),
        pltpu.SemaphoreType.DMA((n_copies,)),
    ]
    vmem, hbm = pl.BlockSpec(memory_space=pltpu.VMEM), pl.BlockSpec(memory_space=pl.ANY)
    return pl.pallas_call(
        kernel,
        out_shape=(
            jax.ShapeDtypeStruct((tok, d), BF),
            jax.ShapeDtypeStruct((tok, d), BF),
            jax.ShapeDtypeStruct((dr, ff), BF),
            jax.ShapeDtypeStruct((dr, ff), BF),
            jax.ShapeDtypeStruct((ff, dr), BF),
        ),
        in_specs=[vmem] * 4 + [hbm] * 3,
        out_specs=(vmem,) * 5,
        scratch_shapes=scratch,
        compiler_params=pltpu.CompilerParams(
            collective_id=0, has_side_effects=True, vmem_limit_bytes=48 * 1024 * 1024
        ),
    )


def local(tokens, routes, route_gates, out_grad, w_gate, w_up, w_down):
    call = build(tokens.shape[0], tokens.shape[1], w_gate.shape[1])
    return call(tokens, routes, route_gates, out_grad, w_gate, w_up, w_down)


def solution(mesh):
    return jax.shard_map(
        local,
        mesh=mesh,
        in_specs=(
            P(("dp", "expert"), None),
            P(("dp", "expert"), None),
            P(("dp", "expert"), None),
            P(("dp", "expert"), None),
            P(None, "expert"),
            P(None, "expert"),
            P("expert", None),
        ),
        out_specs=(
            P(("dp", "expert"), None),
            P(("dp", "expert"), None),
            P("dp", "expert"),
            P("dp", "expert"),
            P("expert", "dp"),
        ),
        check_vma=False,
    )
```

time: 509 us -> 90.5 us (0.18)
  the two profiles are of different devices: /device:TPU:1 before, /device:TPU:4 now
where the time goes in v1:
time: 90.5 us; the launch traced here: 90.1 us
  Pallas kernels  80.4 us (89%)
  local copies, waits for them, and re-layouts  9.04 us (10%)
    pallas_call x1, Pallas kernels, local(): return call(tokens, routes, route_gates, out_grad, w_gate, w_up, w_down)  80.4 us
    unnamed x18, local copies, waits for them, and re-layouts  8.33 us

profile of v1, /device:TPU:4, one launch (start us, length us, event | category | flops | bytes accessed | tf_op | source)
XLA Modules:
  0.0 90.1 jit_solution(14285422422084042979)
XLA Ops:
  0.6 0.0 copy-start.5
  0.6 0.8 copy.12.routes_ref
  1.4 0.0 copy-done.5
  1.4 0.1 copy.13.gates_ref
  1.5 0.0 copy-start
  1.5 1.2 %copy-done = bf16[3584,128]{1,0:T(8,128)(2,1)S(1)} copy-done((bf16[3584,128]{1,0:T(8,128)(2,1)S(1)}, bf16[3584,128]{1,0:T(8,128)(2,1)}, u32[]{:S(2)}) %copy-start) | copy-done | bytes 917528
  2.7 0.0 copy-start.1
  2.7 1.2 %copy-done.1 = bf16[3584,128]{1,0:T(8,128)(2,1)S(1)} copy-done((bf16[3584,128]{1,0:T(8,128)(2,1)S(1)}, bf16[3584,128]{1,0:T(8,128)(2,1)}, u32[]{:S(2)}) %copy-start.1) | copy-done | bytes 917528
  3.9 0.0 copy-start.2
  3.9 1.2 %copy-done.2 = bf16[128,3584]{1,0:T(8,128)(2,1)S(1)} copy-done((bf16[128,3584]{1,0:T(8,128)(2,1)S(1)}, bf16[128,3584]{1,0:T(8,128)(2,1)}, u32[]{:S(2)}) %copy-start.2) | copy-done | bytes 917528
  5.0 0.0 copy-start.3
  5.0 0.7 copy-done.3
  5.8 0.0 copy-start.4
  5.8 0.7 copy-done.4
  6.5 80.4 %shard_map.110 = (bf16[4,3584]{1,0:T(4,128)(2,1)S(1)}, bf16[4,3584]{1,0:T(4,128)(2,1)S(1)}, bf16[112,128]{1,0:T(8,128)(2,1)S(1)}, bf16[112,128]{1,0:T(8,128)(2,1)S(1)}, bf16[128,112]{1,0:T(8,128)(2,1)S(1)}) custom-call(bf16[4,3584]{1,0:T(4,128)(2,1)S(1)} %copy-done.3, s32[4,2]{1,0:T(4,128)S(1)} %copy.12.routes_ref, f32[4,2]{1,0:T(4,128)S(1)} %copy.13.gates_ref, ...), custom_call_target="tpu_custom_call" | custom-call | tf_op jit(solution)/shard_map/pallas_call | solution.py:397
  86.9 0.7 copy.14
  87.7 0.6 copy.19
  88.3 0.6 copy.20
  88.9 0.6 copy.21
  89.5 0.6 copy.22
Async XLA Ops:
  0.6 0.8 copy-start.5
  1.5 1.2 %copy-start = (bf16[3584,128]{1,0:T(8,128)(2,1)S(1)}, bf16[3584,128]{1,0:T(8,128)(2,1)}, u32[]{:S(2)}) copy-start(bf16[3584,128]{1,0:T(8,128)(2,1)} %wg_hbm.1) | copy-start | bytes 2752516
  2.7 1.2 %copy-start.1 = (bf16[3584,128]{1,0:T(8,128)(2,1)S(1)}, bf16[3584,128]{1,0:T(8,128)(2,1)}, u32[]{:S(2)}) copy-start(bf16[3584,128]{1,0:T(8,128)(2,1)} %wu_hbm.1) | copy-start | bytes 2752516
  3.9 1.2 %copy-start.2 = (bf16[128,3584]{1,0:T(8,128)(2,1)S(1)}, bf16[128,3584]{1,0:T(8,128)(2,1)}, u32[]{:S(2)}) copy-start(bf16[128,3584]{1,0:T(8,128)(2,1)} %wd_hbm.1) | copy-start | bytes 2752516
  5.0 0.7 copy-start.3
  5.8 0.7 copy-start.4

commit v2 on v1

--- a/solution.py
+++ b/solution.py
@@ -25,7 +25,7 @@
     return -(-(n // tile) // 2) * tile
 
 
-def build(tok, d, ff):
+def build(tok, d, ff, topk):
     lt, le = tok.bit_length() - 1, EXPERTS.bit_length() - 1
     ly = NY.bit_length() - 1
     seg_w = d // SEG
@@ -42,9 +42,9 @@
     n_copies = 9 * NY + 5 * 2 * hx + NB + 2 * 2 * hz + 4
 
     def kernel(
-        tok_ref, routes_ref, gates_ref, og_ref, wg_hbm, wu_hbm, wd_hbm,
-        out_ref, dx_ref, gg_ref, gu_ref, gd_ref,
-        wgu, wd, xc, dc, gc, xy, dy, gy, xg, dg, gx, sdo,
+        tok_hbm, routes_hbm, gates_hbm, og_hbm, wg_hbm, wu_hbm, wd_hbm,
+        out_ref, dx_ref, grad_ref,
+        tok_ref, routes_ref, gates_ref, og_ref, wgu, wd, xc, dc, gc, xy, dy, gy, xg, dg, gx, sdo,
         o_part, d_part, o_in, d_in, oc, xo, oy, xdy,
         gp, gcin, zsum, zin, hout, hin,
         wsem, ssem, rsem,
@@ -73,6 +73,14 @@
         for p in partners:
             pl.semaphore_signal(barrier, inc=1, device_id=p, device_id_type=pl.DeviceIdType.MESH)
 
+        small = [
+            pltpu.make_async_copy(tok_hbm, tok_ref, wsem.at[3]),
+            pltpu.make_async_copy(routes_hbm, routes_ref, wsem.at[4]),
+            pltpu.make_async_copy(gates_hbm, gates_ref, wsem.at[5]),
+            pltpu.make_async_copy(og_hbm, og_ref, wsem.at[6]),
+        ]
+        for load in small:
+            load.start()
         loads = [
             pltpu.make_async_copy(wg_hbm, wgu.at[:, 0:ff], wsem.at[0]),
             pltpu.make_async_copy(wu_hbm, wgu.at[:, ff : 2 * ff], wsem.at[1]),
@@ -107,13 +115,16 @@
                 total = term if total is None else total + term
             return total.astype(BF)
 
+        small[0].wait()
         xc[...] = pack(tok_ref)
-        lane, row = iota((tok, 128), 1), iota((tok, 128), 0)
-        table = jnp.zeros((tok, 128), F32)
-        for k in range(routes_ref.shape[1]):
-            mine = ((lane >> le) == row) & ((lane & (EXPERTS - 1)) == routes_ref[:, k : k + 1])
-            table = table + jnp.where(mine, gates_ref[:, k : k + 1], 0.0)
-        line = jnp.sum(table, axis=0, keepdims=True)
+        small[1].wait()
+        small[2].wait()
+        lane = iota((1, 128), 1)
+        line = jnp.zeros((1, 128), F32)
+        for k in range(topk):
+            for t in range(tok):
+                mine = lane == t * EXPERTS + routes_ref[k : k + 1, t : t + 1]
+                line = line + jnp.where(mine, gates_ref[k : k + 1, t : t + 1], 0.0)
         gc[...] = jnp.where(iota((8, 128), 0) == y, line, 0.0)
 
         pl.semaphore_wait(barrier, len(partners))
@@ -122,6 +133,7 @@
             send(("yx", k), xc, xy.at[y], at_y((y + k) % NY))
         for k in range(1, NY):
             send(("yg", k), gc, gy.at[y], at_y((y + k) % NY))
+        small[3].wait()
         dc[...] = pack(og_ref)
         for k in range(1, NY):
             send(("yd", k), dc, dy.at[y], at_y((y + k) % NY))
@@ -251,7 +263,7 @@
             zs = pl.ds(((z // zb + order[k]) % NB) * zb, zb)
             return zs, gcin.at[zs]
 
-        for k in range(NB):
+        def grad_block(k):
             block = (z // zb + order[k]) % NB
             cols = pl.ds(pl.multiple_of(block * bw, bw), bw)
             pgu = mm(xg[:, cols], dgu, TN).astype(BF)
@@ -266,9 +278,9 @@
             zs, dst = core_views(k)
             send(("c", k), gp.at[1 - c, zs], dst, other_c)
 
-        for i in range(0, d, kb):
-            d_part[:, i : i + kb] = mm(dgu, wgu[i : i + kb, :], NT).astype(BF)
-        scatter_start("dx", d_part, d_in)
+        def core_arrive(k):
+            zs, dst = core_views(k)
+            arrive(("c", k), dst, other_c)
 
         def both(zd, hh, at):
             return gp[c, zd, hh, at].astype(F32) + gcin[zd, hh, at].astype(F32)
@@ -299,18 +311,24 @@
             total = both(z, hh, every) + zin[k, 0, hz - 1].astype(F32)
             return total + zin[k, 1, hz - 1].astype(F32)
 
-        zs, dst = core_views(0)
-        arrive(("c", 0), dst, other_c)
+        grad_block(0)
+        grad_block(1)
+        scatter_step("o", o_part, o_in, 1)
+        core_arrive(0)
         z_start(0, 1 - h)
         z_start(1, h)
+        for k in range(2, NB):
+            grad_block(k)
+        for i in range(0, d, kb):
+            d_part[:, i : i + kb] = mm(dgu, wgu[i : i + kb, :], NT).astype(BF)
+        scatter_start("dx", d_part, d_in)
         for k in range(1, NB):
-            zs, dst = core_views(k)
-            arrive(("c", k), dst, other_c)
+            core_arrive(k)
 
         for s in range(1, max(hx, hz)):
             if s < hz:
                 z_step(0, 1 - h, s)
-            if s < hx:
+            if 1 < s < hx:
                 scatter_step("o", o_part, o_in, s)
             if s < hz:
                 z_step(1, h, s)
@@ -346,11 +364,7 @@
         line_end("oy", oc, oy, out_ref)
         line_end("xy2", xo, xdy, dx_ref)
         arrive(("h",), hin, other_h)
-        total = (total + hin[...].astype(F32)).astype(BF)
-        gg_ref[...] = total[0:dr]
-        gu_ref[...] = total[dr : 2 * dr]
-        eye = (iota((dr, dr), 0) == iota((dr, dr), 1)).astype(BF)
-        gd_ref[...] = mm(total[2 * dr : gr], eye, TN).astype(BF)
+        grad_ref[...] = (total + hin[...].astype(F32)).astype(BF)
 
         for op in sent:
             op.wait_send()
@@ -360,6 +374,7 @@
         return pltpu.VMEM(shape, dtype)
 
     scratch = [
+        vm((tok, d)), vm((topk, tok), jnp.int32), vm((topk, tok), F32), vm((tok, d)),
         vm((d, 2 * ff)), vm((ff, d)),
         vm((chunk, seg_w)), vm((chunk, seg_w)), vm((8, 128), F32),
         vm((NY, chunk, seg_w)), vm((NY, chunk, seg_w)), vm((NY, 8, 128), F32),
@@ -369,32 +384,46 @@
         vm((NY - 1, chunk, seg_w)), vm((NY - 1, chunk, seg_w)),
         vm((NC, NZ, NH, gr, ff)), vm((NZ, NH, gr, ff)), vm((NZ, NH, gr, ff)),
         vm((2, 2, hz, gr, ff)), vm((gr, ff)), vm((gr, ff)),
-        pltpu.SemaphoreType.DMA((3,)),
+        pltpu.SemaphoreType.DMA((7,)),
         pltpu.SemaphoreType.DMA((n_copies,)),
         pltpu.SemaphoreType.DMA((n_copies,)),
     ]
-    vmem, hbm = pl.BlockSpec(memory_space=pltpu.VMEM), pl.BlockSpec(memory_space=pl.ANY)
-    return pl.pallas_call(
+    vmem, hbm = pl.BlockSpec(memory_space=pltpu.VMEM), pl.BlockSpec(memory_space=pltpu.HBM)
+
+    def write(a, b, g, a2, b2, g0, g1, g2):
+        a2[...] = a[...]
+        b2[...] = b[...]
+        g0[...] = g[0:dr]
+        g1[...] = g[dr : 2 * dr]
+        g2[...] = g[2 * dr : gr]
+
+    rows_out = jax.ShapeDtypeStruct((tok, d), BF)
+    grad_out = jax.ShapeDtypeStruct((dr, ff), BF)
+    main = pl.pallas_call(
         kernel,
-        out_shape=(
-            jax.ShapeDtypeStruct((tok, d), BF),
-            jax.ShapeDtypeStruct((tok, d), BF),
-            jax.ShapeDtypeStruct((dr, ff), BF),
-            jax.ShapeDtypeStruct((dr, ff), BF),
-            jax.ShapeDtypeStruct((ff, dr), BF),
-        ),
-        in_specs=[vmem] * 4 + [hbm] * 3,
-        out_specs=(vmem,) * 5,
+        out_shape=(rows_out, rows_out, jax.ShapeDtypeStruct((gr, ff), BF)),
+        in_specs=[hbm] * 7,
+        out_specs=(vmem,) * 3,
         scratch_shapes=scratch,
         compiler_params=pltpu.CompilerParams(
-            collective_id=0, has_side_effects=True, vmem_limit_bytes=48 * 1024 * 1024
+            collective_id=0, has_side_effects=True, vmem_limit_bytes=60 * 1024 * 1024
         ),
     )
+    last = pl.pallas_call(
+        write,
+        out_shape=(rows_out, rows_out, grad_out, grad_out, grad_out),
+        in_specs=[vmem] * 3,
+        out_specs=(vmem,) * 5,
+        compiler_params=pltpu.CompilerParams(vmem_limit_bytes=60 * 1024 * 1024),
+    )
+    return main, last
 
 
 def local(tokens, routes, route_gates, out_grad, w_gate, w_up, w_down):
-    call = build(tokens.shape[0], tokens.shape[1], w_gate.shape[1])
-    return call(tokens, routes, route_gates, out_grad, w_gate, w_up, w_down)
+    main, last = build(tokens.shape[0], tokens.shape[1], w_gate.shape[1], routes.shape[1])
+    parts = main(tokens, routes.T, route_gates.T, out_grad, w_gate, w_up, w_down)
+    moe_out, token_grad, grad_gate, grad_up, grad_down = last(*parts)
+    return moe_out, token_grad, grad_gate, grad_up, grad_down.T
 
 
 def solution(mesh):

time: 90.5 us -> 83.8 us (0.926)
  the two profiles are of different devices: /device:TPU:4 before, /device:TPU:1 now
where the time goes in v2:
time: 83.8 us; the launch traced here: 83.6 us
  Pallas kernels  83 us (99%)
    pallas_call x1, Pallas kernels, local(): main(tokens, routes.T, route_gates.T, out_grad, w_gate, w_up, w_down)  81.4 us

profile of v2, /device:TPU:1, one launch (start us, length us, event | category | flops | bytes accessed | tf_op | source)
XLA Modules:
  0.0 83.6 jit_solution(3598431523932180528)
XLA Ops:
  0.6 81.4 %shard_map.110 = (bf16[4,3584]{1,0:T(4,128)(2,1)}, bf16[4,3584]{1,0:T(4,128)(2,1)}, bf16[336,128]{1,0:T(8,128)(2,1)}) custom-call(bf16[4,3584]{1,0:T(4,128)(2,1)} %tok_hbm.1, s32[2,4]{1,0:T(2,128)} %bitcast.3, f32[2,4]{1,0:T(2,128)} %bitcast.4, bf16[4,3584]{1,0:T(4,128)(2,1)} %og_hbm.1, bf16[3584,128]{1,0:T(8,128)(2,1)} %wg_hbm.1, bf16[3584,128]{1,0:T(8,128)(2,1)} %wu_hbm.1, ...), custom_call_target="tpu_custom_call" | custom-call | tf_op jit(solution)/shard_map/pallas_call | solution.py:424
  82.0 1.6 %shard_map.111 = (bf16[4,3584]{1,0:T(4,128)(2,1)}, bf16[4,3584]{1,0:T(4,128)(2,1)}, bf16[112,128]{1,0:T(8,128)(2,1)}, bf16[112,128]{1,0:T(8,128)(2,1)}, bf16[112,128]{1,0:T(8,128)(2,1)}) custom-call(bf16[4,3584]{1,0:T(4,128)(2,1)} %get-tuple-element.13.a, bf16[4,3584]{1,0:T(4,128)(2,1)} %get-tuple-element.14.b, bf16[336,128]{1,0:T(8,128)(2,1)} %get-tuple-element.15.g), custom_call_target="tpu_custom_call" | custom-call | tf_op jit(solution)/shard_map/pallas_call | solution.py:425

commit v3 on v2

--- a/solution.py
+++ b/solution.py
@@ -9,6 +9,7 @@
 EXPERTS = 4
 SEG = 4
 NB = 4
+SIDE = 1024
 BF, F32 = jnp.bfloat16, jnp.float32
 NN, NT, TN = (((1,), (0,)), ((), ())), (((1,), (1,)), ((), ())), (((0,), (0,)), ((), ()))
 
@@ -28,7 +29,9 @@
 def build(tok, d, ff, topk):
     lt, le = tok.bit_length() - 1, EXPERTS.bit_length() - 1
     ly = NY.bit_length() - 1
-    seg_w = d // SEG
+    da = d - SIDE
+    seg_w, seg_s, seg_o = da // SEG, SIDE // SEG, d // SEG
+    side = NX * tok
     chunk = SEG * tok
     brow = NY * tok
     rows = NX * brow
@@ -36,17 +39,17 @@
     bw, zb = d // NB, NZ // NB
     dr = d // (NZ * NH * NC)
     gr = 3 * dr
-    ds = split(d, 128)
+    ds, das = split(d, 128), split(da, 128)
     gs = split(gr, 16)
     kb = 512
-    n_copies = 9 * NY + 5 * 2 * hx + NB + 2 * 2 * hz + 4
+    n_copies = 11 * NY + NX + 5 * 2 * hx + NB + 2 * 2 * hz + 4
 
     def kernel(
         tok_hbm, routes_hbm, gates_hbm, og_hbm, wg_hbm, wu_hbm, wd_hbm,
         out_ref, dx_ref, grad_ref,
-        tok_ref, routes_ref, gates_ref, og_ref, wgu, wd, xc, dc, gc, xy, dy, gy, xg, dg, gx, sdo,
+        tok_ref, routes_ref, gates_ref, og_ref, wgu, wd, xc, dc, bc, bx, bm, by, gc, xy, dy, gy, xg, dg, gx, sdo,
         o_part, d_part, o_in, d_in, oc, xo, oy, xdy,
-        gp, gcin, zsum, zin, hout, hin,
+        gp, gcin, zsum, zin, hout, hin, own,
         wsem, ssem, rsem,
     ):
         dp, ei = lax.axis_index("dp"), lax.axis_index("expert")
@@ -67,7 +70,8 @@
         other_h = ((z * NH + 1 - h) * NC + c, ei)
         other_c = ((z * NH + h) * NC + 1 - c, ei)
         partners = [at_y((y + k) % NY) for k in range(1, NY)]
-        partners += [right, left, up, down, other_h, other_c]
+        partners += [at_x((x + k) % NX) for k in range(1, NX)]
+        partners += [up, down, other_h, other_c]
 
         barrier = pltpu.get_barrier_semaphore()
         for p in partners:
@@ -107,16 +111,26 @@
         def arrive(key, dst, dev):
             copy(key, dst, dst, dev).wait_recv()
 
-        def pack(ref):
+        def pack(ref, start, width):
             total = None
             for s in range(SEG):
                 place = (iota((chunk, tok), 0) == iota((chunk, tok), 1) + s * tok).astype(BF)
-                term = mm(place, ref[:, s * seg_w : (s + 1) * seg_w])
+                term = mm(place, ref[:, start + s * width : start + (s + 1) * width])
                 total = term if total is None else total + term
             return total.astype(BF)
 
         small[0].wait()
-        xc[...] = pack(tok_ref)
+        xc[...] = pack(tok_ref, 0, seg_w)
+        pl.semaphore_wait(barrier, len(partners))
+
+
+        for k in range(1, NY):
+            send(("yx", k), xc, xy.at[y], at_y((y + k) % NY))
+        small[3].wait()
+        bc[0:chunk] = pack(tok_ref, da, seg_s)
+        bc[chunk : 2 * chunk] = pack(og_ref, da, seg_s)
+        for k in range(1, NX):
+            send(("bx", k), bc, bx.at[x], at_x((x + k) % NX))
         small[1].wait()
         small[2].wait()
         lane = iota((1, 128), 1)
@@ -127,14 +141,9 @@
                 line = line + jnp.where(mine, gates_ref[k : k + 1, t : t + 1], 0.0)
         gc[...] = jnp.where(iota((8, 128), 0) == y, line, 0.0)
 
-        pl.semaphore_wait(barrier, len(partners))
-
-        for k in range(1, NY):
-            send(("yx", k), xc, xy.at[y], at_y((y + k) % NY))
         for k in range(1, NY):
             send(("yg", k), gc, gy.at[y], at_y((y + k) % NY))
-        small[3].wait()
-        dc[...] = pack(og_ref)
+        dc[...] = pack(og_ref, 0, seg_w)
         for k in range(1, NY):
             send(("yd", k), dc, dy.at[y], at_y((y + k) % NY))
 
@@ -153,7 +162,7 @@
 
         def gather_views(name, s):
             buf = {"x": xg, "d": dg}[name]
-            r_cols, l_cols = (slice(0, ds), slice(ds, d)) if s == hx else (slice(0, d), slice(0, d))
+            r_cols, l_cols = (slice(0, das), slice(das, da)) if s == hx else (slice(0, da), slice(0, da))
             return buf, r_cols, l_cols
 
         def gather_send(name, s):
@@ -193,6 +202,19 @@
             arrive(("yd", k), dy.at[(y + NY - k) % NY], at_y((y + k) % NY))
         unpack_to(dy, dc, dg)
         gather_send("d", 1)
+
+        for k in range(1, NX):
+            arrive(("bx", k), bx.at[(x + NX - k) % NX], at_x((x + k) % NX))
+        bx[pl.ds(x, 1)] = bc[...][None]
+        pieces = bx[...].reshape(NX * 2 * chunk, seg_s)
+        for s in range(SEG):
+            r, q = iota((2 * side, NX * 2 * chunk), 0), iota((2 * side, NX * 2 * chunk), 1)
+            from_x = ((r & (side - 1)) >> lt) * (2 * chunk) + (r >> (side.bit_length() - 1)) * chunk
+            take = (q == from_x + s * tok + (r & (tok - 1))).astype(BF)
+            bm[:, s * seg_s : (s + 1) * seg_s] = mm(take, pieces).astype(BF)
+        for k in range(1, NY):
+            send(("by", k), bm, by.at[y], at_y((y + k) % NY))
+
         for s in range(1, hx):
             gather_arrive("x", s)
             gather_send("x", s + 1)
@@ -200,6 +222,15 @@
             gate_send(s + 1)
             gather_arrive("d", s)
             gather_send("d", s + 1)
+
+        for k in range(1, NY):
+            arrive(("by", k), by.at[(y + NY - k) % NY], at_y((y + k) % NY))
+        by[pl.ds(y, 1)] = bm[...][None]
+        r, q = iota((rows, rows), 0), iota((rows, rows), 1)
+        from_y = ((r >> lt) & (NY - 1)) * side + (r >> (lt + ly)) * tok + (r & (tok - 1))
+        turn = (q == from_y).astype(BF)
+        xg[:, da:d] = mm(turn, by[:, 0:side].reshape(rows, SIDE)).astype(BF)
+        dg[:, da:d] = mm(turn, by[:, side : 2 * side].reshape(rows, SIDE)).astype(BF)
         gather_arrive("x", hx)
         gate_arrive(hx)
 
@@ -311,42 +342,18 @@
             total = both(z, hh, every) + zin[k, 0, hz - 1].astype(F32)
             return total + zin[k, 1, hz - 1].astype(F32)
 
-        grad_block(0)
-        grad_block(1)
-        scatter_step("o", o_part, o_in, 1)
-        core_arrive(0)
-        z_start(0, 1 - h)
-        z_start(1, h)
-        for k in range(2, NB):
-            grad_block(k)
-        for i in range(0, d, kb):
-            d_part[:, i : i + kb] = mm(dgu, wgu[i : i + kb, :], NT).astype(BF)
-        scatter_start("dx", d_part, d_in)
-        for k in range(1, NB):
-            core_arrive(k)
-
-        for s in range(1, max(hx, hz)):
-            if s < hz:
-                z_step(0, 1 - h, s)
-            if 1 < s < hx:
-                scatter_step("o", o_part, o_in, s)
-            if s < hz:
-                z_step(1, h, s)
-            if s < hx:
-                scatter_step("dx", d_part, d_in, s)
-
         def line_start(name, total, pieces, into):
             spread = None
             for s in range(SEG):
-                term = mm(place_of(s), total[:, s * seg_w : (s + 1) * seg_w], TN)
+                term = mm(place_of(s), total[:, s * seg_o : (s + 1) * seg_o], TN)
                 spread = term if spread is None else spread + term
-            pieces[...] = spread.astype(BF).reshape(NY, chunk, seg_w)
+            pieces[...] = spread.astype(BF).reshape(NY, chunk, seg_o)
             for k in range(1, NY):
                 dst_y = (y + k) % NY
                 send((name, k), pieces.at[dst_y], into.at[k - 1], at_y(dst_y))
 
         def line_end(name, pieces, into, result):
-            total = pieces[pl.ds(y, 1)].reshape(chunk, seg_w).astype(F32)
+            total = pieces[pl.ds(y, 1)].reshape(chunk, seg_o).astype(F32)
             for k in range(1, NY):
                 arrive((name, k), into.at[k - 1], at_y((y + k) % NY))
                 total = total + into[k - 1].astype(F32)
@@ -354,17 +361,54 @@
             for s in range(SEG):
                 r, q = iota((chunk, chunk), 0), iota((chunk, chunk), 1)
                 back = ((q == r + s * tok) & (r < tok)).astype(BF)
-                result[:, s * seg_w : (s + 1) * seg_w] = mm(back, total)[0:tok].astype(BF)
-
-        hout[...] = z_end(0, 1 - h).astype(BF)
-        send(("h",), hout, hin, other_h)
+                result[:, s * seg_o : (s + 1) * seg_o] = mm(back, total)[0:tok].astype(BF)
+
+        def dx_products():
+            for i in range(0, d, kb):
+                d_part[:, i : i + kb] = mm(dgu, wgu[i : i + kb, :], NT).astype(BF)
+            scatter_start("dx", d_part, d_in)
+
+        def h_start():
+            hout[...] = z_end(0, 1 - h).astype(BF)
+            send(("h",), hout, hin, other_h)
+
+        def own_end():
+            own[...] = z_end(1, h)
+
+        def h_end():
+            arrive(("h",), hin, other_h)
+            grad_ref[...] = (own[...] + hin[...].astype(F32)).astype(BF)
+
+        dx_products()
+        grad_block(0)
+        grad_block(1)
+        scatter_step("o", o_part, o_in, 1)
+        core_arrive(0)
+        z_start(0, 1 - h)
+        z_start(1, h)
+        grad_block(2)
+        grad_block(3)
+        scatter_step("dx", d_part, d_in, 1)
+        core_arrive(1)
+        core_arrive(2)
+        core_arrive(3)
+        scatter_step("o", o_part, o_in, 2)
+        z_step(0, 1 - h, 1)
+        z_step(1, h, 1)
+        scatter_step("dx", d_part, d_in, 2)
+        z_step(0, 1 - h, 2)
+        scatter_step("o", o_part, o_in, 3)
+        z_step(1, h, 2)
+        scatter_step("dx", d_part, d_in, 3)
+        z_step(0, 1 - h, 3)
+        z_step(1, h, 3)
+        h_start()
         line_start("oy", scatter_end("o", o_part, o_in), oc, oy)
         line_start("xy2", scatter_end("dx", d_part, d_in), xo, xdy)
-        total = z_end(1, h)
+        own_end()
         line_end("oy", oc, oy, out_ref)
         line_end("xy2", xo, xdy, dx_ref)
-        arrive(("h",), hin, other_h)
-        grad_ref[...] = (total + hin[...].astype(F32)).astype(BF)
+        h_end()
 
         for op in sent:
             op.wait_send()
@@ -376,14 +420,16 @@
     scratch = [
         vm((tok, d)), vm((topk, tok), jnp.int32), vm((topk, tok), F32), vm((tok, d)),
         vm((d, 2 * ff)), vm((ff, d)),
-        vm((chunk, seg_w)), vm((chunk, seg_w)), vm((8, 128), F32),
+        vm((chunk, seg_w)), vm((chunk, seg_w)),
+        vm((2 * chunk, seg_s)), vm((NX, 2 * chunk, seg_s)), vm((2 * side, SIDE)), vm((NY, 2 * side, SIDE)),
+        vm((8, 128), F32),
         vm((NY, chunk, seg_w)), vm((NY, chunk, seg_w)), vm((NY, 8, 128), F32),
         vm((rows, d)), vm((rows, d)), vm((NX, 8, 128), F32), vm((rows, d)),
         vm((rows, d)), vm((rows, d)), vm((2, hx, brow, d)), vm((2, hx, brow, d)),
-        vm((NY, chunk, seg_w)), vm((NY, chunk, seg_w)),
-        vm((NY - 1, chunk, seg_w)), vm((NY - 1, chunk, seg_w)),
+        vm((NY, chunk, seg_o)), vm((NY, chunk, seg_o)),
+        vm((NY - 1, chunk, seg_o)), vm((NY - 1, chunk, seg_o)),
         vm((NC, NZ, NH, gr, ff)), vm((NZ, NH, gr, ff)), vm((NZ, NH, gr, ff)),
-        vm((2, 2, hz, gr, ff)), vm((gr, ff)), vm((gr, ff)),
+        vm((2, 2, hz, gr, ff)), vm((gr, ff)), vm((gr, ff)), vm((gr, ff), F32),
         pltpu.SemaphoreType.DMA((7,)),
         pltpu.SemaphoreType.DMA((n_copies,)),
         pltpu.SemaphoreType.DMA((n_copies,)),

time: 83.8 us -> 79.4 us (0.947)
  Pallas kernels: 83 us -> 78.1 us
    pallas_call x1, Pallas kernels: 81.4 us -> 76.5 us  [local(): main(tokens, routes.T, route_gates.T, out_grad, w_gate, w_up, w_down)]
where the time goes in v3:
time: 79.4 us; the launch traced here: 78.8 us
  Pallas kernels  78.1 us (98%)
    pallas_call x1, Pallas kernels, local(): main(tokens, routes.T, route_gates.T, out_grad, w_gate, w_up, w_down)  76.5 us

profile of v3, /device:TPU:1, one launch (start us, length us, event | category | flops | bytes accessed | tf_op | source)
XLA Modules:
  0.0 78.8 jit_solution(12973081780119402000)
XLA Ops:
  0.6 76.5 %shard_map.110 = (bf16[4,3584]{1,0:T(4,128)(2,1)}, bf16[4,3584]{1,0:T(4,128)(2,1)}, bf16[336,128]{1,0:T(8,128)(2,1)}) custom-call(bf16[4,3584]{1,0:T(4,128)(2,1)} %tok_hbm.1, s32[2,4]{1,0:T(2,128)} %bitcast.3, f32[2,4]{1,0:T(2,128)} %bitcast.4, bf16[4,3584]{1,0:T(4,128)(2,1)} %og_hbm.1, bf16[3584,128]{1,0:T(8,128)(2,1)} %wg_hbm.1, bf16[3584,128]{1,0:T(8,128)(2,1)} %wu_hbm.1, ...), custom_call_target="tpu_custom_call" | custom-call | tf_op jit(solution)/shard_map/pallas_call | solution.py:470
  77.2 1.6 %shard_map.111 = (bf16[4,3584]{1,0:T(4,128)(2,1)}, bf16[4,3584]{1,0:T(4,128)(2,1)}, bf16[112,128]{1,0:T(8,128)(2,1)}, bf16[112,128]{1,0:T(8,128)(2,1)}, bf16[112,128]{1,0:T(8,128)(2,1)}) custom-call(bf16[4,3584]{1,0:T(4,128)(2,1)} %get-tuple-element.13.a, bf16[4,3584]{1,0:T(4,128)(2,1)} %get-tuple-element.14.b, bf16[336,128]{1,0:T(8,128)(2,1)} %get-tuple-element.15.g), custom_call_target="tpu_custom_call" | custom-call | tf_op jit(solution)/shard_map/pallas_call | solution.py:471

commit v4 on v3

--- a/solution.py
+++ b/solution.py
@@ -30,7 +30,7 @@
     lt, le = tok.bit_length() - 1, EXPERTS.bit_length() - 1
     ly = NY.bit_length() - 1
     da = d - SIDE
-    seg_w, seg_s, seg_o = da // SEG, SIDE // SEG, d // SEG
+    seg_w, seg_s = da // SEG, SIDE // SEG
     side = NX * tok
     chunk = SEG * tok
     brow = NY * tok
@@ -39,17 +39,17 @@
     bw, zb = d // NB, NZ // NB
     dr = d // (NZ * NH * NC)
     gr = 3 * dr
-    ds, das = split(d, 128), split(da, 128)
+    das = split(da, 128)
     gs = split(gr, 16)
     kb = 512
-    n_copies = 11 * NY + NX + 5 * 2 * hx + NB + 2 * 2 * hz + 4
+    n_copies = 13 * NY + 2 * NX + 5 * 2 * hx + NB + 2 * 2 * hz + 4
 
     def kernel(
         tok_hbm, routes_hbm, gates_hbm, og_hbm, wg_hbm, wu_hbm, wd_hbm,
         out_ref, dx_ref, grad_ref,
         tok_ref, routes_ref, gates_ref, og_ref, wgu, wd, xc, dc, bc, bx, bm, by, gc, xy, dy, gy, xg, dg, gx, sdo,
         o_part, d_part, o_in, d_in, oc, xo, oy, xdy,
-        gp, gcin, zsum, zin, hout, hin, own,
+        gp, gcin, zsum, zin, hout, hin, own, oside, osin, dside, dsin, sout, sin,
         wsem, ssem, rsem,
     ):
         dp, ei = lax.axis_index("dp"), lax.axis_index("expert")
@@ -256,25 +256,36 @@
             o_part[:, i : i + kb] = (mm(hidden, wd[:, i : i + kb]) * gate).astype(BF)
 
         def scatter_start(name, part, into):
-            v = part.at[xrows(x + hx), 0:ds]
-            send((name, "r", 1), v, into.at[0, 0, :, 0:ds], right)
-            v = part.at[xrows(x + hx), ds:d]
-            send((name, "l", 1), v, into.at[1, 0, :, ds:d], left)
+            v = part.at[xrows(x + hx), 0:das]
+            send((name, "r", 1), v, into.at[0, 0, :, 0:das], right)
+            v = part.at[xrows(x + hx), das:da]
+            send((name, "l", 1), v, into.at[1, 0, :, das:da], left)
 
         def scatter_step(name, part, into, s):
             for i, (way, dev) in enumerate((("r", right), ("l", left))):
-                cols = slice(0, d) if s > 1 else slice(ds, d) if i else slice(0, ds)
+                cols = slice(0, da) if s > 1 else slice(das, da) if i else slice(0, das)
                 arrive((name, way, s), into.at[i, s - 1, :, cols], dev)
                 at = xrows(x + hx - s) if i == 0 else xrows(x + NX - hx + s)
                 total = part[at, cols].astype(F32) + into[i, s - 1, :, cols].astype(F32)
                 part[at, cols] = total.astype(BF)
-                send((name, way, s + 1), part.at[at], into.at[i, s], dev)
+                send((name, way, s + 1), part.at[at, 0:da], into.at[i, s], dev)
 
         def scatter_end(name, part, into):
             arrive((name, "r", hx), into.at[0, hx - 1], right)
             arrive((name, "l", hx), into.at[1, hx - 1], left)
-            total = part[xrows(x), :].astype(F32) + into[0, hx - 1].astype(F32)
+            total = part[xrows(x), 0:da].astype(F32) + into[0, hx - 1].astype(F32)
             return (total + into[1, hx - 1].astype(F32)).astype(BF)
+
+        def turn_rows():
+            r, q = iota((rows, rows), 0), iota((rows, rows), 1)
+            from_y = ((r >> lt) & (NY - 1)) * side + (r >> (lt + ly)) * tok + (r & (tok - 1))
+            return (q == from_y).astype(BF)
+
+        def side_start(name, part, mine, into):
+            mine[...] = mm(turn_rows(), part[:, da:d], TN).astype(BF).reshape(NY, side, SIDE)
+            for k in range(1, NY):
+                to = (y + k) % NY
+                send((name, k), mine.at[to], into.at[k - 1], at_y(to))
 
         scatter_start("o", o_part, o_in)
 
@@ -345,23 +356,52 @@
         def line_start(name, total, pieces, into):
             spread = None
             for s in range(SEG):
-                term = mm(place_of(s), total[:, s * seg_o : (s + 1) * seg_o], TN)
+                term = mm(place_of(s), total[:, s * seg_w : (s + 1) * seg_w], TN)
                 spread = term if spread is None else spread + term
-            pieces[...] = spread.astype(BF).reshape(NY, chunk, seg_o)
+            pieces[...] = spread.astype(BF).reshape(NY, chunk, seg_w)
             for k in range(1, NY):
                 dst_y = (y + k) % NY
                 send((name, k), pieces.at[dst_y], into.at[k - 1], at_y(dst_y))
 
         def line_end(name, pieces, into, result):
-            total = pieces[pl.ds(y, 1)].reshape(chunk, seg_o).astype(F32)
+            total = pieces[pl.ds(y, 1)].reshape(chunk, seg_w).astype(F32)
             for k in range(1, NY):
                 arrive((name, k), into.at[k - 1], at_y((y + k) % NY))
                 total = total + into[k - 1].astype(F32)
-            total = total.astype(BF)
+            unstack(total.astype(BF), 0, seg_w, result)
+
+        def unstack(total, start, width, result):
             for s in range(SEG):
                 r, q = iota((chunk, chunk), 0), iota((chunk, chunk), 1)
                 back = ((q == r + s * tok) & (r < tok)).astype(BF)
-                result[:, s * seg_o : (s + 1) * seg_o] = mm(back, total)[0:tok].astype(BF)
+                result[:, start + s * width : start + (s + 1) * width] = mm(back, total)[0:tok].astype(BF)
+
+        def side_turn():
+            for i, (name, mine, into) in enumerate((("os", oside, osin), ("ds", dside, dsin))):
+                total = mine[pl.ds(y, 1)].reshape(side, SIDE).astype(F32)
+                for k in range(1, NY):
+                    arrive((name, k), into.at[k - 1], at_y((y + k) % NY))
+                    total = total + into[k - 1].astype(F32)
+                total = total.astype(BF)
+                spread = None
+                for s in range(SEG):
+                    r, q = iota((NX * chunk, side), 0), iota((NX * chunk, side), 1)
+                    take = (r == (q >> lt) * chunk + s * tok + (q & (tok - 1))).astype(BF)
+                    term = mm(take, total[:, s * seg_s : (s + 1) * seg_s])
+                    spread = term if spread is None else spread + term
+                sout[:, i * chunk : (i + 1) * chunk] = spread.astype(BF).reshape(NX, chunk, seg_s)
+            for k in range(1, NX):
+                to = (x + k) % NX
+                send(("sx", k), sout.at[to], sin.at[k - 1], at_x(to))
+
+        def side_end():
+            total = sout[pl.ds(x, 1)].reshape(2 * chunk, seg_s).astype(F32)
+            for k in range(1, NX):
+                arrive(("sx", k), sin.at[k - 1], at_x((x + k) % NX))
+                total = total + sin[k - 1].astype(F32)
+            total = total.astype(BF)
+            unstack(total[0:chunk], da, seg_s, out_ref)
+            unstack(total[chunk : 2 * chunk], da, seg_s, dx_ref)
 
         def dx_products():
             for i in range(0, d, kb):
@@ -379,6 +419,7 @@
             arrive(("h",), hin, other_h)
             grad_ref[...] = (own[...] + hin[...].astype(F32)).astype(BF)
 
+        side_start("os", o_part, oside, osin)
         dx_products()
         grad_block(0)
         grad_block(1)
@@ -386,6 +427,7 @@
         core_arrive(0)
         z_start(0, 1 - h)
         z_start(1, h)
+        side_start("ds", d_part, dside, dsin)
         grad_block(2)
         grad_block(3)
         scatter_step("dx", d_part, d_in, 1)
@@ -398,16 +440,18 @@
         scatter_step("dx", d_part, d_in, 2)
         z_step(0, 1 - h, 2)
         scatter_step("o", o_part, o_in, 3)
+        z_step(0, 1 - h, 3)
         z_step(1, h, 2)
         scatter_step("dx", d_part, d_in, 3)
-        z_step(0, 1 - h, 3)
-        z_step(1, h, 3)
         h_start()
         line_start("oy", scatter_end("o", o_part, o_in), oc, oy)
+        side_turn()
+        z_step(1, h, 3)
         line_start("xy2", scatter_end("dx", d_part, d_in), xo, xdy)
         own_end()
         line_end("oy", oc, oy, out_ref)
         line_end("xy2", xo, xdy, dx_ref)
+        side_end()
         h_end()
 
         for op in sent:
@@ -425,11 +469,13 @@
         vm((8, 128), F32),
         vm((NY, chunk, seg_w)), vm((NY, chunk, seg_w)), vm((NY, 8, 128), F32),
         vm((rows, d)), vm((rows, d)), vm((NX, 8, 128), F32), vm((rows, d)),
-        vm((rows, d)), vm((rows, d)), vm((2, hx, brow, d)), vm((2, hx, brow, d)),
-        vm((NY, chunk, seg_o)), vm((NY, chunk, seg_o)),
-        vm((NY - 1, chunk, seg_o)), vm((NY - 1, chunk, seg_o)),
+        vm((rows, d)), vm((rows, d)), vm((2, hx, brow, da)), vm((2, hx, brow, da)),
+        vm((NY, chunk, seg_w)), vm((NY, chunk, seg_w)),
+        vm((NY - 1, chunk, seg_w)), vm((NY - 1, chunk, seg_w)),
         vm((NC, NZ, NH, gr, ff)), vm((NZ, NH, gr, ff)), vm((NZ, NH, gr, ff)),
         vm((2, 2, hz, gr, ff)), vm((gr, ff)), vm((gr, ff)), vm((gr, ff), F32),
+        vm((NY, side, SIDE)), vm((NY - 1, side, SIDE)), vm((NY, side, SIDE)), vm((NY - 1, side, SIDE)),
+        vm((NX, 2 * chunk, seg_s)), vm((NX - 1, 2 * chunk, seg_s)),
         pltpu.SemaphoreType.DMA((7,)),
         pltpu.SemaphoreType.DMA((n_copies,)),
         pltpu.SemaphoreType.DMA((n_copies,)),

time: 79.4 us -> 78.4 us (0.987)
  the two profiles are of different devices: /device:TPU:1 before, /device:TPU:16 now
where the time goes in v4:
time: 78.4 us; the launch traced here: 78.2 us
  Pallas kernels  77.5 us (99%)
    pallas_call x1, Pallas kernels, local(): main(tokens, routes.T, route_gates.T, out_grad, w_gate, w_up, w_down)  75.9 us
    pallas_call x1, Pallas kernels, local(): moe_out, token_grad, grad_gate, grad_up, grad_down = last(*parts)  1.58 us

profile of v4, /device:TPU:16, one launch (start us, length us, event | category | flops | bytes accessed | tf_op | source)
XLA Modules:
  0.0 78.2 jit_solution(18673837530543927)
XLA Ops:
  0.6 75.9 %shard_map.110 = (bf16[4,3584]{1,0:T(4,128)(2,1)}, bf16[4,3584]{1,0:T(4,128)(2,1)}, bf16[336,128]{1,0:T(8,128)(2,1)}) custom-call(bf16[4,3584]{1,0:T(4,128)(2,1)} %tok_hbm.1, s32[2,4]{1,0:T(2,128)} %bitcast.3, f32[2,4]{1,0:T(2,128)} %bitcast.4, bf16[4,3584]{1,0:T(4,128)(2,1)} %og_hbm.1, bf16[3584,128]{1,0:T(8,128)(2,1)} %wg_hbm.1, bf16[3584,128]{1,0:T(8,128)(2,1)} %wu_hbm.1, ...), custom_call_target="tpu_custom_call" | custom-call | tf_op jit(solution)/shard_map/pallas_call | solution.py:516
  76.6 1.6 %shard_map.111 = (bf16[4,3584]{1,0:T(4,128)(2,1)}, bf16[4,3584]{1,0:T(4,128)(2,1)}, bf16[112,128]{1,0:T(8,128)(2,1)}, bf16[112,128]{1,0:T(8,128)(2,1)}, bf16[112,128]{1,0:T(8,128)(2,1)}) custom-call(bf16[4,3584]{1,0:T(4,128)(2,1)} %get-tuple-element.13.a, bf16[4,3584]{1,0:T(4,128)(2,1)} %get-tuple-element.14.b, bf16[336,128]{1,0:T(8,128)(2,1)} %get-tuple-element.15.g), custom_call_target="tpu_custom_call" | custom-call | tf_op jit(solution)/shard_map/pallas_call | solution.py:517
